TPU v7x, 512 devices: a whole 4x8x8 slice. The times are simulated.
512 devices in a mesh: cfg: 2 (over y_hi), seq: 32 (over z, y_lo), blk: 8 (over x, core).
Axes of the slice: x: 4, y: 8 (y_hi: 2, y_lo: 4; y = y_hi * 4 + y_lo), z: 8, core: 2. Of those that a mesh axis runs over, the one named last changes fastest.
Arguments:
- tokens_in: bfloat16 [2, 4096, 1536], P('cfg', 'seq'), may hold values from -6 to 6
- modulation: float32 [2, 8, 1536], replicated, may hold values from -3 to 3
- qk_gain: float32 [2, 64], replicated, as said below
- qkv_weight: bfloat16 [3, 1536, 1536], P(None, 'blk'), may hold values from -0.15625 to 0.15625
- out_weight: bfloat16 [1536, 1536], P('blk'), may hold values from -0.15625 to 0.15625
- up_weight: bfloat16 [1536, 6144], P('seq', 'blk'), may hold values from -0.15625 to 0.15625
- down_weight: bfloat16 [6144, 1536], P('blk', 'seq'), may hold values from -0.078125 to 0.078125
- proj_weight: bfloat16 [1536, 64], replicated, may hold values from -0.15625 to 0.15625
- latent: float32 [4096, 64], P(('seq', 'blk'), 'cfg'), may hold values from -6 to 6
- text_count: int32 [1], replicated, may hold values from 64 to 2047
- positions: int32 [3, 4096], P(None, 'seq'), may hold values from 0 to 47
- step_index: int32 [1], replicated, may hold values from 20 to 999
- guidance: float32 [1], replicated, may hold values from 4 to 8
Outputs:
- hidden_out: bfloat16 [2, 4096, 1536], P('cfg', ('seq', 'blk'))
- latent_prev: float32 [4096, 64], P(('seq', 'blk'), 'cfg')
Inputs may be any that keep to these rules, and one draw needn't show every extreme that they name: `qk_gain`: positive gains.
All inputs are finite; a program needn't handle non-finite values.
Results may differ from a plain program's by a relative error of at most 0.015.
The roundings to bfloat16 on the way count: a program that leaves them out, or rounds other values in their place, can miss the bound.
Values may be sent and summed in bfloat16 or wider, within the bound.
No kernel may reach another device: no remote copies, remote signals or barrier semaphores. Data moves between devices by JAX's collectives and lax.ppermute only.
A program may use at most 64 MiB of HBM per device.

v0:
```python
import math
import jax
import jax.numpy as jnp
from jax import lax
from jax.sharding import PartitionSpec as P

HEAD = 64
STRIDE = 20
rope_bands = (16, 24, 24)


def swapped(block, axis, stride):
    count = lax.axis_size(axis)
    route = []
    for low in range(count):
        high = low | 1 << stride
        if high != low and high < count:
            route += [(low, high), (high, low)]
    return lax.ppermute(block, axis, route)


def layer_norm(values, epsilon):
    average = jnp.mean(values, -1, keepdims=True)
    centered = values - average
    spread = jnp.mean(centered * centered, -1, keepdims=True)
    return centered * lax.rsqrt(spread + epsilon)


def pick_mods(modulation, is_video, which):
    return jnp.where(
        is_video[:, None], modulation[1, which][None, :], modulation[0, which][None, :]
    )


def modulate(values, modulation, is_video, shift_row, scale_row):
    normed = layer_norm(values, 1e-05)
    return normed * (1.0 + pick_mods(modulation, is_video, scale_row)) + pick_mods(
        modulation, is_video, shift_row
    )


def rope_tables(positions, is_video):
    angle_parts = []
    for axis_pos, band_width in enumerate(rope_bands):
        exponent = jnp.arange(band_width // 2, dtype=jnp.float32) * (2.0 / band_width)
        inverse = jnp.exp(-exponent * math.log(10000.0))
        angle_parts.append(positions[axis_pos].astype(jnp.float32)[:, None] * inverse[None, :])
    angles = jnp.concatenate(angle_parts, 1) * is_video.astype(jnp.float32)[:, None]
    return (jnp.cos(angles), jnp.sin(angles))


def rotate(vectors, cosine, sine):
    pieces = []
    offset = 0
    half_offset = 0
    for band_width in rope_bands:
        half_width = band_width // 2
        first_half = vectors[..., offset : offset + half_width]
        second = vectors[..., offset + half_width : offset + band_width]
        cos_band = cosine[:, None, half_offset : half_offset + half_width]
        sin_band = sine[:, None, half_offset : half_offset + half_width]
        pieces.append(first_half * cos_band - second * sin_band)
        pieces.append(second * cos_band + first_half * sin_band)
        offset = offset + band_width
        half_offset = half_offset + half_width
    return jnp.concatenate(pieces, -1)


def head_prep(flat_heads, gain, cosine, sine):
    token_count = flat_heads.shape[0]
    shaped = flat_heads.reshape(token_count, -1, HEAD)
    normed = layer_norm(shaped, 1e-06) * gain[None, None, :]
    turned = rotate(normed, cosine, sine)
    return turned.reshape(token_count, -1).astype(jnp.bfloat16)


def ddim_update(latent, guided, step_index):
    steps_all = jnp.arange(1000, dtype=jnp.float32)
    root_beta = math.sqrt(0.00085) + steps_all / 999.0 * (math.sqrt(0.012) - math.sqrt(0.00085))
    alpha_bar = jnp.exp(jnp.cumsum(jnp.log1p(-root_beta * root_beta)))
    indices = jnp.arange(1000, dtype=jnp.int32)
    alpha_now = jnp.sum(jnp.where(indices == step_index[0], alpha_bar, 0.0))
    alpha_prev = jnp.sum(jnp.where(indices == step_index[0] - STRIDE, alpha_bar, 0.0))
    clean_est = jnp.sqrt(alpha_now) * latent - jnp.sqrt(1.0 - alpha_now) * guided
    noise_est = jnp.sqrt(1.0 - alpha_now) * latent + jnp.sqrt(alpha_now) * guided
    return jnp.sqrt(alpha_prev) * clean_est + jnp.sqrt(1.0 - alpha_prev) * noise_est


def body(
    tokens_in,
    modulation,
    qk_gain,
    qkv_weight,
    out_weight,
    up_weight,
    down_weight,
    proj_weight,
    latent,
    text_count,
    positions,
    step_index,
    guidance,
):
    row_count = tokens_in.shape[1]
    own_count = row_count // lax.axis_size("blk")
    blk_index = lax.axis_index("blk")
    token_ids = lax.axis_index("seq") * row_count + jnp.arange(row_count, dtype=jnp.int32)
    is_video = token_ids >= text_count[0]
    own_video = lax.dynamic_slice_in_dim(is_video, blk_index * own_count, own_count, 0)
    residual = tokens_in[0].astype(jnp.float32)
    cosine, sine = rope_tables(positions, is_video)
    normed = modulate(residual, modulation, is_video, 0, 1).astype(jnp.bfloat16)
    projected = jnp.einsum("td,ked->kte", normed, qkv_weight, preferred_element_type=jnp.float32)
    head_count = projected.shape[2] // HEAD
    queries = head_prep(projected[0], qk_gain[0], cosine, sine)
    keys_local = head_prep(projected[1], qk_gain[1], cosine, sine)
    values_local = projected[2].astype(jnp.bfloat16)
    query_heads = queries.reshape(row_count, head_count, HEAD)
    initial = (
        jnp.full((head_count, row_count), -1e30, jnp.float32),
        jnp.zeros((head_count, row_count), jnp.float32),
        jnp.zeros((head_count, row_count, HEAD), jnp.float32),
    )
    key_piece = lax.all_gather(keys_local, "seq", axis=0, tiled=True)
    value_piece = lax.all_gather(values_local, "seq", axis=0, tiled=True)
    piece_len = key_piece.shape[0]
    key_blocks = key_piece.reshape(piece_len // piece_len, piece_len, head_count, HEAD)
    value_blocks = value_piece.reshape(piece_len // piece_len, piece_len, head_count, HEAD)

    def absorb_block(state, key_value):
        key_block, value_block = key_value
        running_max, running_sum, weighted = state
        scores = (
            jnp.einsum("thd,shd->hts", query_heads, key_block, preferred_element_type=jnp.float32)
            * 0.125
        )
        new_max = jnp.maximum(running_max, jnp.max(scores, -1))
        rescale = jnp.exp(running_max - new_max)
        weights = jnp.exp(scores - new_max[..., None])
        running_sum = running_sum * rescale + jnp.sum(weights, -1)
        weighted = weighted * rescale[..., None] + jnp.einsum(
            "hts,shd->htd",
            weights.astype(jnp.bfloat16),
            value_block,
            preferred_element_type=jnp.float32,
        )
        return ((new_max, running_sum, weighted), None)

    state, unused = lax.scan(absorb_block, initial, (key_blocks, value_blocks))
    running_max, running_sum, weighted = state
    attn_out = (
        (weighted / running_sum[..., None])
        .transpose(1, 0, 2)
        .reshape(row_count, head_count * HEAD)
        .astype(jnp.bfloat16)
    )
    attn_proj = lax.psum(
        jnp.dot(attn_out, out_weight, preferred_element_type=jnp.float32).astype(jnp.bfloat16),
        "blk",
    ).astype(jnp.float32)
    after_attn = residual + pick_mods(modulation, is_video, 2) * attn_proj
    normed_mlp = modulate(after_attn, modulation, is_video, 3, 4).astype(jnp.bfloat16)
    own_after = lax.dynamic_slice_in_dim(after_attn, blk_index * own_count, own_count, 0)
    up_full, down_full = (
        lax.all_gather(up_weight, "seq", axis=0, tiled=True),
        lax.all_gather(down_weight, "seq", axis=1, tiled=True),
    )
    hidden_up = jnp.dot(normed_mlp, up_full, preferred_element_type=jnp.float32)
    activated = jax.nn.gelu(hidden_up, approximate=True).astype(jnp.bfloat16)
    mlp_part = jnp.dot(activated, down_full, preferred_element_type=jnp.float32)
    mlp_rows = lax.psum_scatter(
        mlp_part.astype(jnp.bfloat16), "blk", scatter_dimension=0, tiled=True
    ).astype(jnp.float32)
    after_mlp = own_after + pick_mods(modulation, own_video, 5) * mlp_rows
    hidden_out = after_mlp.astype(jnp.bfloat16)[None]
    final_norm = modulate(after_mlp, modulation, own_video, 6, 7).astype(jnp.bfloat16)
    predicted = jnp.dot(final_norm, proj_weight, preferred_element_type=jnp.float32)
    half_width = latent.shape[1]
    branch_index = lax.axis_index("cfg")
    kept = lax.dynamic_slice_in_dim(predicted, branch_index * half_width, half_width, 1)
    outgoing = lax.dynamic_slice_in_dim(predicted, (1 - branch_index) * half_width, half_width, 1)
    partner = swapped(outgoing, "cfg", 0)
    is_cond = branch_index == 0
    cond_pred = jnp.where(is_cond, kept, partner)
    uncond_pred = jnp.where(is_cond, partner, kept)
    guided = uncond_pred + guidance[0] * (cond_pred - uncond_pred)
    latent_prev = ddim_update(latent, guided, step_index)
    return (hidden_out, latent_prev)


def solution(mesh):
    in_specs = (
        P("cfg", "seq", None),
        P(),
        P(),
        P(None, "blk", None),
        P("blk", None),
        P("seq", "blk"),
        P("blk", "seq"),
        P(),
        P(("seq", "blk"), "cfg"),
        P(),
        P(None, "seq"),
        P(),
        P(),
    )
    out_specs = (P("cfg", ("seq", "blk"), None), P(("seq", "blk"), "cfg"))
    return jax.shard_map(body, mesh=mesh, in_specs=in_specs, out_specs=out_specs, check_vma=False)
```

profile of v0, /device:TPU:64, one launch (start us, length us, event | category | flops | bytes accessed | tf_op | source)
XLA Modules:
  0.0 744.4 jit_solution(7766577091344267166)
XLA Ops:
  7.2 0.0 all-gather.6.cloned.1.call-start
  8.0 0.8 convert_bitcast_fusion.4
  8.8 0.1 broadcast_multiply_fusion.2
  8.9 0.1 broadcast_multiply_fusion.1
  9.0 0.1 fusion.74
  9.1 1.8 slice_reduce_fusion.3
  10.9 1.1 convert_reduce_fusion
  12.0 1.3 fusion.21
  13.3 1.7 convolution_bitcast_fusion
  15.3 0.1 multiply_multiply_fusion.1
  15.4 5.1 concatenate.13
  20.5 0.0 all-gather.6.cloned.1.call-update
  20.5 0.0 all-gather.12.cloned.1.call-start
  20.6 0.6 slice.262
  21.2 0.1 all-gather.12.cloned.1.call-update
  21.3 0.0 all-reduce.3.cloned.1.call-start
  21.4 0.3 concatenate.12
  21.7 134.0 %all-gather.6.cloned.1.call-done = bf16[4096,192]{0,1:T(8,128)(2,1)} async-done(((bf16[128,192]{0,1:T(8,128)(2,1)}), bf16[4096,192]{0,1:T(8,128)(2,1)}) %all-gather.6.cloned.1.call-update) | async-done | bytes 1572880 | tf_op jit(solution)/shard_map/all_gather | solution.py:124
  155.6 2.5 fusion.90
  158.2 1.0 fusion
  159.1 1.7 copy-done.1
  160.8 124.8 %all-gather.12.cloned.1.call-done = bf16[1,4096,192]{1,2,0:T(8,128)(2,1)} async-done(((bf16[1,128,192]{1,2,0:T(8,128)(2,1)}), bf16[1,4096,192]{1,2,0:T(8,128)(2,1)}) %all-gather.12.cloned.1.call-update) | async-done | bytes 1572880 | tf_op jit(solution)/shard_map/all_gather | solution.py:125
  285.6 4.6 fusion.14
  290.3 1.1 convolution_convert_fusion.1
  291.3 0.0 all-gather.10.cloned.1.call-start
  291.4 0.5 all-gather.10.cloned.1.call-update
  291.9 0.0 all-gather.8.cloned.1.call-start
  292.0 0.5 all-gather.8.cloned.1.call-update
  292.5 0.0 reduce-scatter.2.cloned.1.call-start
  292.6 66.6 %all-reduce.3.cloned.1.call-done = bf16[128,1536]{1,0:T(8,128)(2,1)} async-done(((bf16[128,1536]{1,0:T(8,128)(2,1)}), bf16[128,1536]{1,0:T(8,128)(2,1)}) %all-reduce.3.cloned.1.call-update) | async-done | bytes 393232 | tf_op jit(solution)/shard_map/psum | solution.py:157
  359.1 1.3 fusion.84
  360.4 0.2 multiply_reduce_fusion
  360.7 154.4 %all-gather.10.cloned.1.call-done = bf16[768,1536]{0,1:T(8,128)(2,1)} async-done(((bf16[768,48]{0,1:T(8,128)(2,1)}), bf16[768,1536]{0,1:T(8,128)(2,1)}) %all-gather.10.cloned.1.call-update) | async-done | bytes 2359312 | tf_op jit(solution)/shard_map/all_gather | solution.py:166
  515.1 162.1 %all-gather.8.cloned.1.call-done = bf16[1536,768]{1,0:T(8,128)(2,1)} async-done(((bf16[48,768]{1,0:T(8,128)(2,1)}), bf16[1536,768]{1,0:T(8,128)(2,1)}) %all-gather.8.cloned.1.call-update) | async-done | bytes 2359312 | tf_op jit(solution)/shard_map/all_gather | solution.py:165
  677.3 4.5 convolution_convert_fusion
  681.8 0.1 dynamic_slice.18
  681.9 0.3 reduce-window.9
  682.2 0.1 slice.181
  683.0 0.1 slice_reduce_fusion.16
  683.1 0.1 add_bitcast_fusion
  683.1 40.3 %reduce-scatter.2.cloned.1.call-done = bf16[16,1536]{1,0:T(8,128)(2,1)} async-done(((bf16[128,1536]{1,0:T(8,128)(2,1)}), bf16[16,1536]{1,0:T(8,128)(2,1)}) %reduce-scatter.2.cloned.1.call-update) | async-done | bytes 49168 | tf_op jit(solution)/shard_map/reduce_scatter | solution.py:171
  723.4 1.0 fusion.83
  724.4 0.7 multiply_reduce_fusion.1
  725.2 0.2 fusion.64
  725.4 0.1 constant_dynamic-slice_fusion
  725.5 7.4 collective-permute-start
  732.9 0.7 select_reduce_fusion
  736.9 0.7 multiply_add_fusion.1
  (46 shorter events, 0.4 us)
Async XLA Ops:
  7.2 6.2 copy-start
  7.2 148.4 %all-gather.6.cloned.1.call-start = ((), (), s32[]{:S(2)}) async-start(), calls=%async_computation.1 | async-start | bytes 1622016 | tf_op jit(solution)/shard_map/all_gather | solution.py:124
  12.0 3.2 copy-start.5
  20.5 265.1 %all-gather.12.cloned.1.call-start = ((), (), s32[]{:S(2)}) async-start(), calls=%async_computation.6 | async-start | bytes 1622016 | tf_op jit(solution)/shard_map/all_gather | solution.py:125
  21.3 337.8 %all-reduce.3.cloned.1.call-start = ((), (), s32[]{:S(2)}) async-start(), calls=%async_computation.2 | async-start | bytes 786432 | tf_op jit(solution)/shard_map/psum | solution.py:157
  158.1 2.7 copy-start.1
  285.6 4.6 copy-start.3
  285.6 73.5 %copy-start.2 = (bf16[1,128,1536]{2,1,0:T(8,128)(2,1)S(1)}, bf16[1,128,1536]{2,1,0:T(8,128)(2,1)}, u32[]{:S(2)}) copy-start(bf16[1,128,1536]{2,1,0:T(8,128)(2,1)} %param.13) | copy-start | bytes 1179652
  291.3 223.8 %all-gather.10.cloned.1.call-start = ((), (), s32[]{:S(2)}) async-start(), calls=%async_computation.4 | async-start | bytes 2433024 | tf_op jit(solution)/shard_map/all_gather | solution.py:166
  291.9 385.3 %all-gather.8.cloned.1.call-start = ((), (), s32[]{:S(2)}) async-start(), calls=%async_computation.3 | async-start | bytes 2433024 | tf_op jit(solution)/shard_map/all_gather | solution.py:165
  292.5 430.9 %reduce-scatter.2.cloned.1.call-start = ((), (), s32[]{:S(2)}) async-start(), calls=%async_computation.5 | async-start | bytes 442368 | tf_op jit(solution)/shard_map/reduce_scatter | solution.py:171
  677.3 47.9 %copy-start.6 = (bf16[1536,64]{0,1:T(8,128)(2,1)S(1)}, bf16[1536,64]{0,1:T(8,128)(2,1)}, u32[]{:S(2)}) copy-start(bf16[1536,64]{0,1:T(8,128)(2,1)} %param.20) | copy-start | bytes 589828
  677.3 59.6 %copy-start.4 = (f32[16,32]{1,0:T(8,128)S(1)}, f32[16,32]{1,0:T(8,128)}, u32[]{:S(2)}) copy-start(f32[16,32]{1,0:T(8,128)} %param.21) | copy-start | bytes 6148
  725.5 11.4 %collective-permute-start = (f32[16,32]{1,0:T(8,128)S(1)}, f32[16,32]{1,0:T(8,128)S(1)}, u32[]{:S(2)}, u32[]{:S(2)}) collective-permute-start(f32[16,32]{1,0:T(8,128)S(1)} %constant_dynamic-slice_fusion), channel_id=1, source_target_pairs={{0,256},{256,0},{1,257},{257,1},{2,258},{258,2},{3,259},{259,3},{4... | collective-permute-start | bytes 6152 | tf_op jit(solution)/shard_map/ppermute | solution.py:19
Sparse Core Ops, SparseCore 0:
  20.7 134.9 all-gather.5
  158.2 127.3 all-gather.11
  291.5 67.6 all-reduce.2
  361.3 153.8 all-gather.9
  517.2 159.9 all-gather.7
  681.9 41.4 reduce-scatter.1
where the time goes:
time: 745 us; the launch traced here: 744 us
  waiting for transfers between devices  683 us (92%)
  between operations  19.1 us (3%)
  matrix products  14.7 us (2%)
  local copies, waits for them, and re-layouts  9.89 us (1%)
  other arithmetic  9.82 us (1%)
  starting transfers between devices  7.61 us (1%)
    all_gather x1, waiting for transfers between devices, body(): lax.all_gather(up_weight, 'seq', axis=0, tiled=True)  162 us
    all_gather x1, waiting for transfers between devices, body(): lax.all_gather(down_weight, 'seq', axis=1, tiled=True)  154 us
    all_gather x1, waiting for transfers between devices, body(): key_piece = lax.all_gather(keys_local, 'seq', axis=0, tiled=True)  134 us
    all_gather x1, waiting for transfers between devices, body(): value_piece = lax.all_gather(values_local, 'seq', axis=0, tiled=True)  125 us
    psum x1, waiting for transfers between devices, body(): lax.psum(jnp.dot(attn_out, out_weight, preferred_element_type=jnp.float32...  66.6 us
    reduce_scatter x1, waiting for transfers between devices, body(): lax.psum_scatter(mlp_part.astype(jnp.bfloat16), 'blk', scatter_dimension=...  40.3 us
  transfers between devices with their start and end apart: 7, of which 6 were waited for; matrix products, arithmetic and copies ran while one was open for 1% of the time, Pallas kernels for 0%

commit v1 on v0

--- a/solution.py
+++ b/solution.py
@@ -121,7 +121,8 @@
         jnp.zeros((head_count, row_count), jnp.float32),
         jnp.zeros((head_count, row_count, HEAD), jnp.float32),
     )
-    key_piece = lax.all_gather(keys_local, "seq", axis=0, tiled=True)
+    sent = jnp.stack([keys_local] * lax.axis_size("seq"))
+    key_piece = jnp.concatenate(lax.all_to_all(sent, "seq", 0, 0), axis=0)
     value_piece = lax.all_gather(values_local, "seq", axis=0, tiled=True)
     piece_len = key_piece.shape[0]
     key_blocks = key_piece.reshape(piece_len // piece_len, piece_len, head_count, HEAD)

time: 745 us -> 634 us (0.85)
  waiting for transfers between devices: 683 us -> 554 us
  starting transfers between devices: 7.61 us -> 20.7 us
    all_gather x1 -> x0, waiting for transfers between devices: 134 us -> none  [body(): key_piece = lax.all_gather(keys_local, 'seq', axis=0, tiled=True)]
    all_to_all x0 -> x1, waiting for transfers between devices: none -> 40.5 us  [body(): key_piece = jnp.concatenate(lax.all_to_all(sent, 'seq', 0, 0), axis=0)]
    all_gather x1, waiting for transfers between devices: 125 us -> 88.1 us  [body(): value_piece = lax.all_gather(values_local, 'seq', axis=0, tiled=True)]
    all_to_all x0 -> x1, starting transfers between devices: none -> 13.2 us  [body(): key_piece = jnp.concatenate(lax.all_to_all(sent, 'seq', 0, 0), axis=0)]
    all_gather x1, waiting for transfers between devices: 154 us -> 162 us  [body(): lax.all_gather(down_weight, 'seq', axis=1, tiled=True)]
    all_gather x1, waiting for transfers between devices: 162 us -> 155 us  [body(): lax.all_gather(up_weight, 'seq', axis=0, tiled=True)]
  transfers between devices with their start and end apart: 7 -> 7, of which waited for: 6 -> 6; matrix products, arithmetic and copies ran while one was open for 1% -> 2% of each run, Pallas kernels for 0% -> 0%
where the time goes in v1:
time: 634 us; the launch traced here: 633 us
  waiting for transfers between devices  554 us (87%)
  starting transfers between devices  20.7 us (3%)
  between operations  19.1 us (3%)
  local copies, waits for them, and re-layouts  15 us (2%)
  matrix products  13.2 us (2%)
  other arithmetic  10.4 us (2%)
    all_gather x1, waiting for transfers between devices, body(): lax.all_gather(down_weight, 'seq', axis=1, tiled=True)  162 us
    all_gather x1, waiting for transfers between devices, body(): lax.all_gather(up_weight, 'seq', axis=0, tiled=True)  155 us
    all_gather x1, waiting for transfers between devices, body(): value_piece = lax.all_gather(values_local, 'seq', axis=0, tiled=True)  88.1 us
    psum x1, waiting for transfers between devices, body(): lax.psum(jnp.dot(attn_out, out_weight, preferred_element_type=jnp.float32...  67.7 us
    all_to_all x1, waiting for transfers between devices, body(): key_piece = jnp.concatenate(lax.all_to_all(sent, 'seq', 0, 0), axis=0)  40.5 us
    reduce_scatter x1, waiting for transfers between devices, body(): lax.psum_scatter(mlp_part.astype(jnp.bfloat16), 'blk', scatter_dimension=...  40.3 us
    all_to_all x1, starting transfers between devices, body(): key_piece = jnp.concatenate(lax.all_to_all(sent, 'seq', 0, 0), axis=0)  13.2 us
  transfers between devices with their start and end apart: 7, of which 6 were waited for; matrix products, arithmetic and copies ran while one was open for 2% of the time, Pallas kernels for 0%

profile of v1, /device:TPU:64, one launch (start us, length us, event | category | flops | bytes accessed | tf_op | source)
XLA Modules:
  0.0 632.9 jit_solution(10879350506995949987)
XLA Ops:
  8.0 0.8 convert_bitcast_fusion.4
  8.8 0.1 broadcast_multiply_fusion.2
  8.9 0.1 broadcast_multiply_fusion.1
  8.9 0.1 fusion.74
  9.1 2.4 slice_reduce_fusion.3
  11.5 1.1 convert_reduce_fusion
  12.6 1.3 fusion.21
  13.9 1.7 convolution_bitcast_fusion
  15.7 0.7 copy-done.4
  16.6 0.1 multiply_multiply_fusion.1
  16.7 0.6 add_convert_fusion.12
  17.3 0.3 concatenate.13
  17.6 1.5 stack.2
  19.1 13.2 %all-to-all-start = ((bf16[32,128,192]{1,2,0:T(8,128)(2,1)}), bf16[32,128,192]{1,2,0:T(8,128)(2,1)S(1)}, u32[]{:S(2)}, u32[]{:S(2)}) async-start(bf16[32,128,192]{1,2,0:T(8,128)(2,1)} %stack.2), calls=%async_computation | async-start | bytes 3145728 | tf_op jit(solution)/shard_map/all_to_all | solution.py:125
  32.3 0.0 all-gather.9.cloned.1.call-start
  32.3 1.5 slice.262
  33.9 0.0 all-reduce.3.cloned.1.call-start
  34.0 1.7 concatenate.12
  35.6 40.5 %all-to-all-done = bf16[32,128,192]{1,2,0:T(8,128)(2,1)S(1)} async-done(((bf16[32,128,192]{1,2,0:T(8,128)(2,1)}), bf16[32,128,192]{1,2,0:T(8,128)(2,1)S(1)}, u32[]{:S(2)}, u32[]{:S(2)}) %all-to-all-start) | async-done | bytes 1572896 | tf_op jit(solution)/shard_map/all_to_all | solution.py:125
  76.1 2.2 copy.15
  78.3 2.5 squeeze.25
  80.8 1.1 fusion.90
  81.9 1.0 fusion
  82.9 1.7 copy-done.1
  84.6 88.1 %all-gather.9.cloned.1.call-done = bf16[1,4096,192]{1,2,0:T(8,128)(2,1)} async-done(((bf16[1,128,192]{1,2,0:T(8,128)(2,1)}), bf16[1,4096,192]{1,2,0:T(8,128)(2,1)}) %all-gather.9.cloned.1.call-update) | async-done | bytes 1572880 | tf_op jit(solution)/shard_map/all_gather | solution.py:126
  172.7 4.6 fusion.14
  177.3 1.1 convolution_convert_fusion.1
  178.4 0.7 all-gather.5.cloned.1.call-update
  179.2 0.5 all-gather.7.cloned.1.call-update
  179.8 67.7 %all-reduce.3.cloned.1.call-done = bf16[128,1536]{1,0:T(8,128)(2,1)} async-done(((bf16[128,1536]{1,0:T(8,128)(2,1)}), bf16[128,1536]{1,0:T(8,128)(2,1)}) %all-reduce.3.cloned.1.call-update) | async-done | bytes 393232 | tf_op jit(solution)/shard_map/psum | solution.py:158
  247.4 1.3 fusion.84
  248.8 0.2 multiply_reduce_fusion
  249.0 154.6 %all-gather.5.cloned.1.call-done = bf16[1536,768]{1,0:T(8,128)(2,1)} async-done(((bf16[48,768]{1,0:T(8,128)(2,1)}), bf16[1536,768]{1,0:T(8,128)(2,1)}) %all-gather.5.cloned.1.call-update) | async-done | bytes 2359312 | tf_op jit(solution)/shard_map/all_gather | solution.py:166
  403.6 162.1 %all-gather.7.cloned.1.call-done = bf16[768,1536]{0,1:T(8,128)(2,1)} async-done(((bf16[768,48]{0,1:T(8,128)(2,1)}), bf16[768,1536]{0,1:T(8,128)(2,1)}) %all-gather.7.cloned.1.call-update) | async-done | bytes 2359312 | tf_op jit(solution)/shard_map/all_gather | solution.py:167
  565.8 4.5 convolution_convert_fusion
  570.4 0.1 dynamic_slice.18
  570.5 0.3 reduce-window.9
  570.7 0.1 slice.181
  571.5 0.1 slice_reduce_fusion.16
  571.6 0.1 add_bitcast_fusion
  571.7 40.3 %reduce-scatter.2.cloned.1.call-done = bf16[16,1536]{1,0:T(8,128)(2,1)} async-done(((bf16[128,1536]{1,0:T(8,128)(2,1)}), bf16[16,1536]{1,0:T(8,128)(2,1)}) %reduce-scatter.2.cloned.1.call-update) | async-done | bytes 49168 | tf_op jit(solution)/shard_map/reduce_scatter | solution.py:172
  612.0 1.0 fusion.83
  613.0 0.7 multiply_reduce_fusion.1
  613.8 0.2 fusion.64
  614.0 0.1 constant_dynamic-slice_fusion
  614.1 7.4 %collective-permute-start = (f32[16,32]{1,0:T(8,128)S(1)}, f32[16,32]{1,0:T(8,128)S(1)}, u32[]{:S(2)}, u32[]{:S(2)}) collective-permute-start(f32[16,32]{1,0:T(8,128)S(1)} %constant_dynamic-slice_fusion), channel_id=1, source_target_pairs={{0,256},{256,0},{1,257},{257,1},{2,258},{258,2},{3,259},{259,3},{4... | collective-permute-start | bytes 6152 | tf_op jit(solution)/shard_map/ppermute | solution.py:19
  621.4 0.7 select_reduce_fusion
  625.7 0.7 multiply_add_fusion.1
  (70 shorter events, 0.6 us)
Async XLA Ops:
  7.2 6.7 %copy-start = (bf16[3,192,1536]{2,1,0:T(8,128)(2,1)S(1)}, bf16[3,192,1536]{2,1,0:T(8,128)(2,1)}, u32[]{:S(2)}) copy-start(bf16[3,192,1536]{2,1,0:T(8,128)(2,1)} %param.16) | copy-start | bytes 5308420
  8.8 6.9 %copy-start.14 = (pred[128]{0:T(512)(128)(4,1)}, pred[128]{0:T(512)(128)(4,1)S(1)}, u32[]{:S(2)}) copy-start(pred[128]{0:T(512)(128)(4,1)S(1)} %get-tuple-element.46) | copy-start | bytes 388
  12.6 3.9 copy-start.16
  15.7 0.7 copy-start.4
  19.1 57.0 %all-to-all-start = ((bf16[32,128,192]{1,2,0:T(8,128)(2,1)}), bf16[32,128,192]{1,2,0:T(8,128)(2,1)S(1)}, u32[]{:S(2)}, u32[]{:S(2)}) async-start(bf16[32,128,192]{1,2,0:T(8,128)(2,1)} %stack.2), calls=%async_computation | async-start | bytes 3145728 | tf_op jit(solution)/shard_map/all_to_all | solution.py:125
  32.3 140.4 %all-gather.9.cloned.1.call-start = ((), (), s32[]{:S(2)}) async-start(), calls=%async_computation.6 | async-start | bytes 1622016 | tf_op jit(solution)/shard_map/all_gather | solution.py:126
  33.9 213.6 %all-reduce.3.cloned.1.call-start = ((), (), s32[]{:S(2)}) async-start(), calls=%async_computation.2 | async-start | bytes 786432 | tf_op jit(solution)/shard_map/psum | solution.py:158
  81.9 2.7 copy-start.1
  172.7 4.7 copy-start.3
  172.7 74.8 %copy-start.2 = (bf16[1,128,1536]{2,1,0:T(8,128)(2,1)S(1)}, bf16[1,128,1536]{2,1,0:T(8,128)(2,1)}, u32[]{:S(2)}) copy-start(bf16[1,128,1536]{2,1,0:T(8,128)(2,1)} %param.13) | copy-start | bytes 1179652
  172.7 74.8 %copy-start.15 = (pred[128]{0:T(512)(128)(4,1)S(1)}, pred[128]{0:T(512)(128)(4,1)}, u32[]{:S(2)}) copy-start(pred[128]{0:T(512)(128)(4,1)} %copy-done.14) | copy-start | bytes 388
  177.3 388.5 %copy-start.9 = (f32[1536]{0:T(1024)S(1)}, f32[1536]{0:T(1024)}, u32[]{:S(2)}) copy-start(f32[1536]{0:T(1024)} %get-tuple-element.18) | copy-start | bytes 18436
  177.3 388.5 %copy-start.10 = (f32[1536]{0:T(1024)S(1)}, f32[1536]{0:T(1024)}, u32[]{:S(2)}) copy-start(f32[1536]{0:T(1024)} %get-tuple-element.19) | copy-start | bytes 18436
  177.3 388.4 %copy-start.11 = (f32[1536]{0:T(1024)S(1)}, f32[1536]{0:T(1024)}, u32[]{:S(2)}) copy-start(f32[1536]{0:T(1024)} %get-tuple-element.20) | copy-start | bytes 18436
  177.3 388.4 %copy-start.12 = (f32[1536]{0:T(1024)S(1)}, f32[1536]{0:T(1024)}, u32[]{:S(2)}) copy-start(f32[1536]{0:T(1024)} %get-tuple-element.28) | copy-start | bytes 18436
  178.4 225.2 %all-gather.5.cloned.1.call-start = ((), (), s32[]{:S(2)}) async-start(), calls=%async_computation.3 | async-start | bytes 2433024 | tf_op jit(solution)/shard_map/all_gather | solution.py:166
  179.1 386.6 %all-gather.7.cloned.1.call-start = ((), (), s32[]{:S(2)}) async-start(), calls=%async_computation.4 | async-start | bytes 2433024 | tf_op jit(solution)/shard_map/all_gather | solution.py:167
  179.7 432.2 %reduce-scatter.2.cloned.1.call-start = ((), (), s32[]{:S(2)}) async-start(), calls=%async_computation.5 | async-start | bytes 442368 | tf_op jit(solution)/shard_map/reduce_scatter | solution.py:172
  565.7 48.0 %copy-start.5 = (f32[1536]{0:T(1024)S(1)}, f32[1536]{0:T(1024)}, u32[]{:S(2)}) copy-start(f32[1536]{0:T(1024)} %get-tuple-element.16) | copy-start | bytes 18436
  565.8 48.0 %copy-start.6 = (f32[1536]{0:T(1024)S(1)}, f32[1536]{0:T(1024)}, u32[]{:S(2)}) copy-start(f32[1536]{0:T(1024)} %get-tuple-element.17) | copy-start | bytes 18436
  565.8 48.0 %copy-start.7 = (f32[1536]{0:T(1024)S(1)}, f32[1536]{0:T(1024)}, u32[]{:S(2)}) copy-start(f32[1536]{0:T(1024)} %get-tuple-element.37) | copy-start | bytes 18436
  565.8 48.0 %copy-start.8 = (f32[1536]{0:T(1024)S(1)}, f32[1536]{0:T(1024)}, u32[]{:S(2)}) copy-start(f32[1536]{0:T(1024)} %get-tuple-element.38) | copy-start | bytes 18436
  565.8 48.0 %copy-start.17 = (bf16[1536,64]{0,1:T(8,128)(2,1)S(1)}, bf16[1536,64]{0,1:T(8,128)(2,1)}, u32[]{:S(2)}) copy-start(bf16[1536,64]{0,1:T(8,128)(2,1)} %param.20) | copy-start | bytes 589828
  565.8 59.8 %copy-start.13 = (f32[16,32]{1,0:T(8,128)S(1)}, f32[16,32]{1,0:T(8,128)}, u32[]{:S(2)}) copy-start(f32[16,32]{1,0:T(8,128)} %param.21) | copy-start | bytes 6148
  614.1 11.6 %collective-permute-start = (f32[16,32]{1,0:T(8,128)S(1)}, f32[16,32]{1,0:T(8,128)S(1)}, u32[]{:S(2)}, u32[]{:S(2)}) collective-permute-start(f32[16,32]{1,0:T(8,128)S(1)} %constant_dynamic-slice_fusion), channel_id=1, source_target_pairs={{0,256},{256,0},{1,257},{257,1},{2,258},{258,2},{3,259},{259,3},{4... | collective-permute-start | bytes 6152 | tf_op jit(solution)/shard_map/ppermute | solution.py:19
Sparse Core Ops, SparseCore 0:
  35.7 136.9 all-gather.8
  178.5 68.8 all-reduce.2
  249.7 153.8 all-gather.4
  405.7 159.9 all-gather.6
  570.5 41.4 reduce-scatter.1
